TPU v7x, 256 devices: a whole 4x4x8 slice. The times are simulated.
256 devices in a mesh: section: 16 (over z_hi, y), dp: 16 (over x, z_lo, core).
Axes of the slice: x: 4, y: 4, z: 8 (z_hi: 4, z_lo: 2; z = z_hi * 2 + z_lo), core: 2. Of those that a mesh axis runs over, the one named last changes fastest.
Arguments:
- acts: bfloat16 [16, 4, 512, 4096], P('section', None, 'dp'), may hold values from -6 to 6
- out_grad: bfloat16 [4, 512, 4096], P(None, 'dp'), may hold values from -6 to 6
- w_in: bfloat16 [16, 4096, 1152], P('section', 'dp'), may hold values from -0.09375 to 0.09375
- w_out: bfloat16 [16, 4096, 384], P('section', 'dp'), may hold values from -0.09375 to 0.09375
- decay_rate: float32 [16, 3], P('section'), may hold values from 0.004 to 0.04
- cycle_order: int32 [16], replicated, may hold values from 0 to 15, each once
Outputs:
- in_grad: bfloat16 [16, 4, 512, 4096], P('section', None, 'dp')
- grad_in: float32 [16, 4096, 1152], P('section', 'dp')
- grad_out: float32 [16, 4096, 384], P('section', 'dp')
Inputs may be any that keep to these rules, and one draw needn't show every extreme that they name: `cycle_order`: a permutation of the 16 replicas.
All inputs are finite; a program needn't handle non-finite values.
Results may differ from a plain program's by a relative error of at most 0.038.
Values may be sent and summed in bfloat16 or wider, within the bound.
A program may use at most 192 MiB of HBM per device.

v0:
```python
import jax
import jax.numpy as jnp
from jax import lax
from jax.sharding import PartitionSpec as P


def shifted(value, axis, steps):
    count = lax.axis_size(axis)
    initial, last = (max(0, -steps), min(count, count - steps))
    return lax.ppermute(value, axis, [(source, source + steps) for source in range(initial, last)])


def decay_table(rates, length):
    spots = jnp.arange(length).astype(jnp.float32)
    offset = spots[:, None] - spots[None, :]
    decayed = jnp.exp(-rates[:, None, None] * jnp.maximum(offset, 0.0)[None])
    return jnp.where(offset[None] >= 0.0, decayed, 0.0)


def contract_rows(left, right):
    return lax.dot_general(
        left, right, (((0,), (0,)), ((), ())), preferred_element_type=jnp.float32
    )


def contract_cols(left, right):
    return lax.dot_general(
        left, right, (((1,), (1,)), ((), ())), preferred_element_type=jnp.float32
    )


def retention_back(inputs, grad_y, weight_in, weight_out, table):
    length = inputs.shape[0]
    cols = weight_out.shape[1]
    heads = table.shape[0]
    head_size = cols // heads
    qkv = jnp.dot(inputs, weight_in, preferred_element_type=jnp.float32).astype(jnp.bfloat16)
    query = qkv[:, :cols].reshape(length, heads, head_size)
    keys = qkv[:, cols : 2 * cols].reshape(length, heads, head_size)
    values = qkv[:, 2 * cols :].reshape(length, heads, head_size)
    scores = (
        jnp.einsum("the,jhe->htj", query, keys, preferred_element_type=jnp.float32)
        * table
        / head_size
    ).astype(jnp.bfloat16)
    mixed = jnp.einsum("htj,jhe->the", scores, values, preferred_element_type=jnp.float32)
    mixed = mixed.reshape(length, cols).astype(jnp.bfloat16)
    d_mixed = jnp.dot(grad_y, weight_out, preferred_element_type=jnp.float32).astype(jnp.bfloat16)
    d_heads = d_mixed.reshape(length, heads, head_size)
    d_scores = (
        jnp.einsum("the,jhe->htj", d_heads, values, preferred_element_type=jnp.float32)
        * table
        / head_size
    ).astype(jnp.bfloat16)
    d_query = jnp.einsum("htj,jhe->the", d_scores, keys, preferred_element_type=jnp.float32)
    d_keys = jnp.einsum("htj,the->jhe", d_scores, query, preferred_element_type=jnp.float32)
    d_values = jnp.einsum("htj,the->jhe", scores, d_heads, preferred_element_type=jnp.float32)
    d_all = jnp.concatenate(
        [
            d_query.reshape(length, cols),
            d_keys.reshape(length, cols),
            d_values.reshape(length, cols),
        ],
        axis=1,
    ).astype(jnp.bfloat16)
    d_input = (grad_y.astype(jnp.float32) + contract_cols(d_all, weight_in)).astype(jnp.bfloat16)
    return (d_input, d_all, mixed)


def store(buffer, value, which, active):
    older = lax.dynamic_index_in_dim(buffer, which, 0, keepdims=False)
    return lax.dynamic_update_index_in_dim(buffer, jnp.where(active, value, older), which, 0)


def pass_back(d_input):
    return shifted(d_input, "section", -1)


def shards(acts, out_grad, w_in, w_out, decay_rate, cycle_order):
    sections = lax.axis_size("section")
    replicas = lax.axis_size("dp")
    place = lax.axis_index("section")
    replica = lax.axis_index("dp")
    full_in, full_out = (
        lax.all_gather(w_in[0], "dp", axis=0, tiled=True),
        lax.all_gather(w_out[0], "dp", axis=0, tiled=True),
    )
    micro = acts.shape[1]
    length = acts.shape[2]
    width = acts.shape[3]
    cols = full_out.shape[1]
    table = decay_table(decay_rate[0], length)
    saved = acts[0]
    live = jnp.where(replica == cycle_order[replicas - 1], 0.0, 1.0).astype(jnp.float32)
    last_section = sections - 1
    total_steps = micro + sections - 1

    def select(step):
        which = step - (last_section - place)
        active = jnp.logical_and(which >= 0, which < micro)
        return (jnp.clip(which, 0, micro - 1), active)

    def section_input(incoming, which):
        start_grad = lax.dynamic_index_in_dim(out_grad, which, 0, keepdims=False)
        return jnp.where(place == last_section, start_grad, incoming)

    def blank():
        return (
            jnp.zeros((length, width), jnp.bfloat16),
            jnp.zeros((length, 3 * cols), jnp.bfloat16),
            jnp.zeros((length, cols), jnp.bfloat16),
        )

    incoming0 = jnp.zeros((length, width), jnp.bfloat16)
    in_grads0 = jnp.zeros((micro, length, width), jnp.bfloat16)

    def advance(step, carry):
        incoming, in_grads, d_alls, mixes, grad_ys = carry
        which, active = select(step)
        grad_y = section_input(incoming, which)
        inputs = lax.dynamic_index_in_dim(saved, which, 0, keepdims=False)
        d_input, d_all, mixed = lax.cond(
            active, lambda: retention_back(inputs, grad_y, full_in, full_out, table), blank
        )
        in_grads = store(in_grads, d_input, which, active)
        d_alls = store(d_alls, d_all, which, active)
        mixes = store(mixes, mixed, which, active)
        grad_ys = store(grad_ys, grad_y, which, active)
        incoming = pass_back(d_input)
        return (incoming, in_grads, d_alls, mixes, grad_ys)

    start = (
        incoming0,
        in_grads0,
        jnp.zeros((micro, length, 3 * cols), jnp.bfloat16),
        jnp.zeros((micro, length, cols), jnp.bfloat16),
        jnp.zeros((micro, length, width), jnp.bfloat16),
    )
    _, in_grads, d_alls, mixes, grad_ys = lax.fori_loop(0, total_steps, advance, start)
    flat_inputs = saved.reshape(micro * length, width)
    flat_grads = grad_ys.reshape(micro * length, width)
    flat_dall = d_alls.reshape(micro * length, 3 * cols)
    flat_mixed = mixes.reshape(micro * length, cols)
    left_part = contract_rows(flat_inputs, flat_dall)
    right_part = contract_rows(flat_grads, flat_mixed)
    summed = lax.psum_scatter(
        (jnp.concatenate([left_part, right_part], axis=1) * live).astype(jnp.bfloat16),
        "dp",
        scatter_dimension=0,
        tiled=True,
    ).astype(jnp.float32)
    scale = 1.0 / (replicas - 1.0)
    grad_in = (summed[:, : 3 * cols] * scale)[None]
    grad_out = (summed[:, 3 * cols :] * scale)[None]
    return (in_grads[None], grad_in, grad_out)


def solution(mesh):
    placed = (
        P("section", None, "dp", None),
        P(None, "dp", None),
        P("section", "dp", None),
        P("section", "dp", None),
        P("section", None),
        P(),
    )
    return jax.shard_map(
        shards,
        mesh=mesh,
        in_specs=placed,
        out_specs=(
            P("section", None, "dp", None),
            P("section", "dp", None),
            P("section", "dp", None),
        ),
        check_vma=False,
    )
```

profile of v0, /device:TPU:8, one launch (start us, length us, event | category | flops | bytes accessed | tf_op | source)
XLA Modules:
  0.0 765.3 jit_solution(17528883123188055466)
XLA Ops:
  8.7 1.2 slice.21
  11.4 39.7 %all-gather.7.cloned.1.call-done = bf16[1,4096,384]{2,1,0:T(8,128)(2,1)} async-done(((bf16[1,256,384]{2,1,0:T(8,128)(2,1)}), bf16[1,4096,384]{2,1,0:T(8,128)(2,1)}) %all-gather.7.cloned.1.call-update) | async-done | bytes 3145744 | tf_op jit(solution)/shard_map/all_gather | solution.py:86
  51.1 61.7 %all-gather.5.cloned.1.call-done = bf16[1,4096,1152]{2,1,0:T(8,128)(2,1)} async-done(((bf16[1,256,1152]{2,1,0:T(8,128)(2,1)}), bf16[1,4096,1152]{2,1,0:T(8,128)(2,1)}) %all-gather.5.cloned.1.call-update) | async-done | bytes 9437200 | tf_op jit(solution)/shard_map/all_gather | solution.py:85
  113.1 490.0 %while.24 = (s32[]{:T(128)}, bf16[32,4096]{1,0:T(8,128)(2,1)S(1)}, bf16[4,32,4096]{2,1,0:T(8,128)(2,1)S(1)}, bf16[4,32,1152]{2,1,0:T(8,128)(2,1)S(1)}, bf16[4,32...) while((s32[]{:T(128)}, bf16[32,4096]{1,0:T(8,128)(2,1)S(1)}, ...), condition=%wide.region_3.4_spmd.clone, body=%wide.region_0.3_spmd.clone.sunk | while | flops 710326272 | bytes 56925164 | solution.py:139
  113.1 1.1 bitcast_dynamic-update-slice_fusion.11
  114.9 2.4 collective-permute-start
  117.6 7.7 %collective-permute-done = bf16[32,4096]{1,0:T(8,128)(2,1)S(1)} collective-permute-done((bf16[32,4096]{1,0:T(8,128)(2,1)S(1)}, bf16[32,4096]{1,0:T(8,128)(2,1)S(1)}, u32[]{:S(2)}, u32[]{:S(2)}) %collective-permute-start) | collective-permute-done | bytes 262176 | tf_op jit(solution)/shard_map/while/body/eval_jaxpr/ppermute | solution.py:10
  127.0 2.4 collective-permute-start
  129.7 6.9 collective-permute-done
  138.4 2.4 collective-permute-start
  141.0 14.1 %collective-permute-done = bf16[32,4096]{1,0:T(8,128)(2,1)S(1)} collective-permute-done((bf16[32,4096]{1,0:T(8,128)(2,1)S(1)}, bf16[32,4096]{1,0:T(8,128)(2,1)S(1)}, u32[]{:S(2)}, u32[]{:S(2)}) %collective-permute-start) | collective-permute-done | bytes 262176 | tf_op jit(solution)/shard_map/while/body/eval_jaxpr/ppermute | solution.py:10
  156.9 1.9 collective-permute-start
  159.1 13.8 %collective-permute-done = bf16[32,4096]{1,0:T(8,128)(2,1)S(1)} collective-permute-done((bf16[32,4096]{1,0:T(8,128)(2,1)S(1)}, bf16[32,4096]{1,0:T(8,128)(2,1)S(1)}, u32[]{:S(2)}, u32[]{:S(2)}) %collective-permute-start) | collective-permute-done | bytes 262176 | tf_op jit(solution)/shard_map/while/body/eval_jaxpr/ppermute | solution.py:10
  174.7 1.9 collective-permute-start
  176.8 9.2 %collective-permute-done = bf16[32,4096]{1,0:T(8,128)(2,1)S(1)} collective-permute-done((bf16[32,4096]{1,0:T(8,128)(2,1)S(1)}, bf16[32,4096]{1,0:T(8,128)(2,1)S(1)}, u32[]{:S(2)}, u32[]{:S(2)}) %collective-permute-start) | collective-permute-done | bytes 262176 | tf_op jit(solution)/shard_map/while/body/eval_jaxpr/ppermute | solution.py:10
  187.8 1.9 collective-permute-start
  189.9 8.6 %collective-permute-done = bf16[32,4096]{1,0:T(8,128)(2,1)S(1)} collective-permute-done((bf16[32,4096]{1,0:T(8,128)(2,1)S(1)}, bf16[32,4096]{1,0:T(8,128)(2,1)S(1)}, u32[]{:S(2)}, u32[]{:S(2)}) %collective-permute-start) | collective-permute-done | bytes 262176 | tf_op jit(solution)/shard_map/while/body/eval_jaxpr/ppermute | solution.py:10
  200.3 1.9 collective-permute-start
  202.4 8.8 %collective-permute-done = bf16[32,4096]{1,0:T(8,128)(2,1)S(1)} collective-permute-done((bf16[32,4096]{1,0:T(8,128)(2,1)S(1)}, bf16[32,4096]{1,0:T(8,128)(2,1)S(1)}, u32[]{:S(2)}, u32[]{:S(2)}) %collective-permute-start) | collective-permute-done | bytes 262176 | tf_op jit(solution)/shard_map/while/body/eval_jaxpr/ppermute | solution.py:10
  213.1 1.9 collective-permute-start
  215.2 9.2 %collective-permute-done = bf16[32,4096]{1,0:T(8,128)(2,1)S(1)} collective-permute-done((bf16[32,4096]{1,0:T(8,128)(2,1)S(1)}, bf16[32,4096]{1,0:T(8,128)(2,1)S(1)}, u32[]{:S(2)}, u32[]{:S(2)}) %collective-permute-start) | collective-permute-done | bytes 262176 | tf_op jit(solution)/shard_map/while/body/eval_jaxpr/ppermute | solution.py:10
  226.2 1.9 collective-permute-start
  228.3 12.6 %collective-permute-done = bf16[32,4096]{1,0:T(8,128)(2,1)S(1)} collective-permute-done((bf16[32,4096]{1,0:T(8,128)(2,1)S(1)}, bf16[32,4096]{1,0:T(8,128)(2,1)S(1)}, u32[]{:S(2)}, u32[]{:S(2)}) %collective-permute-start) | collective-permute-done | bytes 262176 | tf_op jit(solution)/shard_map/while/body/eval_jaxpr/ppermute | solution.py:10
  242.8 1.9 collective-permute-start
  244.9 13.2 %collective-permute-done = bf16[32,4096]{1,0:T(8,128)(2,1)S(1)} collective-permute-done((bf16[32,4096]{1,0:T(8,128)(2,1)S(1)}, bf16[32,4096]{1,0:T(8,128)(2,1)S(1)}, u32[]{:S(2)}, u32[]{:S(2)}) %collective-permute-start) | collective-permute-done | bytes 262176 | tf_op jit(solution)/shard_map/while/body/eval_jaxpr/ppermute | solution.py:10
  259.9 1.9 collective-permute-start
  262.0 15.0 %collective-permute-done = bf16[32,4096]{1,0:T(8,128)(2,1)S(1)} collective-permute-done((bf16[32,4096]{1,0:T(8,128)(2,1)S(1)}, bf16[32,4096]{1,0:T(8,128)(2,1)S(1)}, u32[]{:S(2)}, u32[]{:S(2)}) %collective-permute-start) | collective-permute-done | bytes 262176 | tf_op jit(solution)/shard_map/while/body/eval_jaxpr/ppermute | solution.py:10
  278.8 1.9 collective-permute-start
  281.0 11.1 %collective-permute-done = bf16[32,4096]{1,0:T(8,128)(2,1)S(1)} collective-permute-done((bf16[32,4096]{1,0:T(8,128)(2,1)S(1)}, bf16[32,4096]{1,0:T(8,128)(2,1)S(1)}, u32[]{:S(2)}, u32[]{:S(2)}) %collective-permute-start) | collective-permute-done | bytes 262176 | tf_op jit(solution)/shard_map/while/body/eval_jaxpr/ppermute | solution.py:10
  293.8 1.9 collective-permute-start
  296.0 8.9 %collective-permute-done = bf16[32,4096]{1,0:T(8,128)(2,1)S(1)} collective-permute-done((bf16[32,4096]{1,0:T(8,128)(2,1)S(1)}, bf16[32,4096]{1,0:T(8,128)(2,1)S(1)}, u32[]{:S(2)}, u32[]{:S(2)}) %collective-permute-start) | collective-permute-done | bytes 262176 | tf_op jit(solution)/shard_map/while/body/eval_jaxpr/ppermute | solution.py:10
  306.7 1.9 collective-permute-start
  308.8 149.8 %collective-permute-done = bf16[32,4096]{1,0:T(8,128)(2,1)S(1)} collective-permute-done((bf16[32,4096]{1,0:T(8,128)(2,1)S(1)}, bf16[32,4096]{1,0:T(8,128)(2,1)S(1)}, u32[]{:S(2)}, u32[]{:S(2)}) %collective-permute-start) | collective-permute-done | bytes 262176 | tf_op jit(solution)/shard_map/while/body/eval_jaxpr/ppermute | solution.py:10
  459.7 14.7 %conditional.3 = (bf16[32,4096]{1,0:T(8,128)(2,1)S(1)}, bf16[32,1152]{1,0:T(8,128)(2,1)}, bf16[32,384]{1,0:T(8,128)(2,1)S(1)}) conditional(s32[]{:T(128)} %convert_element_type.90, () %tuple.68, (bf16[32,4096]{1,0:T(8,128)(2,1)S(1)}, bf16[4,32,4096]{2,1,0:T(8,128)(2,1)}, s32[]{:T(128)}, bf16[4096,1152]{1,0:T(8,128)(2,1)}, ...), branch_computations={%region_1.1_spmd, %region_2.2_spmd.clone} | conditional | flops 709883904 | bytes 52238968 | solution.py:122
  459.7 2.6 fusion.7
  462.4 5.5 convolution_convert_fusion
  470.7 3.8 fusion.2
  474.5 1.9 collective-permute-start
  477.5 9.5 %collective-permute-done = bf16[32,4096]{1,0:T(8,128)(2,1)S(1)} collective-permute-done((bf16[32,4096]{1,0:T(8,128)(2,1)S(1)}, bf16[32,4096]{1,0:T(8,128)(2,1)S(1)}, u32[]{:S(2)}, u32[]{:S(2)}) %collective-permute-start) | collective-permute-done | bytes 262176 | tf_op jit(solution)/shard_map/while/body/eval_jaxpr/ppermute | solution.py:10
  488.0 14.7 %conditional.3 = (bf16[32,4096]{1,0:T(8,128)(2,1)S(1)}, bf16[32,1152]{1,0:T(8,128)(2,1)}, bf16[32,384]{1,0:T(8,128)(2,1)S(1)}) conditional(s32[]{:T(128)} %convert_element_type.90, () %tuple.68, (bf16[32,4096]{1,0:T(8,128)(2,1)S(1)}, bf16[4,32,4096]{2,1,0:T(8,128)(2,1)}, s32[]{:T(128)}, bf16[4096,1152]{1,0:T(8,128)(2,1)}, ...), branch_computations={%region_1.1_spmd, %region_2.2_spmd.clone} | conditional | flops 709883904 | bytes 52238968 | solution.py:122
  488.1 2.6 fusion.7
  490.7 5.5 convolution_convert_fusion
  499.0 3.8 fusion.2
  502.8 1.9 collective-permute-start
  505.8 17.3 %collective-permute-done = bf16[32,4096]{1,0:T(8,128)(2,1)S(1)} collective-permute-done((bf16[32,4096]{1,0:T(8,128)(2,1)S(1)}, bf16[32,4096]{1,0:T(8,128)(2,1)S(1)}, u32[]{:S(2)}, u32[]{:S(2)}) %collective-permute-start) | collective-permute-done | bytes 262176 | tf_op jit(solution)/shard_map/while/body/eval_jaxpr/ppermute | solution.py:10
  524.2 14.7 %conditional.3 = (bf16[32,4096]{1,0:T(8,128)(2,1)S(1)}, bf16[32,1152]{1,0:T(8,128)(2,1)}, bf16[32,384]{1,0:T(8,128)(2,1)S(1)}) conditional(s32[]{:T(128)} %convert_element_type.90, () %tuple.68, (bf16[32,4096]{1,0:T(8,128)(2,1)S(1)}, bf16[4,32,4096]{2,1,0:T(8,128)(2,1)}, s32[]{:T(128)}, bf16[4096,1152]{1,0:T(8,128)(2,1)}, ...), branch_computations={%region_1.1_spmd, %region_2.2_spmd.clone} | conditional | flops 709883904 | bytes 52238968 | solution.py:122
  524.2 2.6 fusion.7
  526.8 5.5 convolution_convert_fusion
  535.2 3.8 fusion.2
  538.9 1.9 collective-permute-start
  542.0 15.3 %collective-permute-done = bf16[32,4096]{1,0:T(8,128)(2,1)S(1)} collective-permute-done((bf16[32,4096]{1,0:T(8,128)(2,1)S(1)}, bf16[32,4096]{1,0:T(8,128)(2,1)S(1)}, u32[]{:S(2)}, u32[]{:S(2)}) %collective-permute-start) | collective-permute-done | bytes 262176 | tf_op jit(solution)/shard_map/while/body/eval_jaxpr/ppermute | solution.py:10
  558.4 14.7 %conditional.3 = (bf16[32,4096]{1,0:T(8,128)(2,1)S(1)}, bf16[32,1152]{1,0:T(8,128)(2,1)}, bf16[32,384]{1,0:T(8,128)(2,1)S(1)}) conditional(s32[]{:T(128)} %convert_element_type.90, () %tuple.68, (bf16[32,4096]{1,0:T(8,128)(2,1)S(1)}, bf16[4,32,4096]{2,1,0:T(8,128)(2,1)}, s32[]{:T(128)}, bf16[4096,1152]{1,0:T(8,128)(2,1)}, ...), branch_computations={%region_1.1_spmd, %region_2.2_spmd.clone} | conditional | flops 709883904 | bytes 52238968 | solution.py:122
  558.4 2.6 fusion.7
  561.0 5.5 convolution_convert_fusion
  569.3 3.8 fusion.2
  573.1 1.9 collective-permute-start
  576.1 5.2 collective-permute-done
  583.2 16.0 %collective-permute-start = (bf16[32,4096]{1,0:T(8,128)(2,1)S(1)}, bf16[32,4096]{1,0:T(8,128)(2,1)S(1)}, u32[]{:S(2)}, u32[]{:S(2)}) collective-permute-start(bf16[32,4096]{1,0:T(8,128)(2,1)S(1)} %get-tuple-element.528), channel_id=1, source_target_pairs={{16,0},{32,16},{48,32},{64,48},{80,64},{96,80},{112,96},{128,112},... | collective-permute-start | bytes 786440 | tf_op jit(solution)/shard_map/while/body/eval_jaxpr/ppermute | solution.py:10
  599.4 3.6 collective-permute-done
  604.0 3.9 convolution_bitcast_fusion
  607.9 9.0 %fusion.32 = bf16[4096,1536]{0,1:T(8,128)(2,1)} fusion(f32[4096,384]{0,1:T(8,128)S(1)} %convolution_bitcast_fusion.1, f32[4096,1152]{0,1:T(8,128)S(1)} %convolution_bitcast_fusion, f32[]{:T(128)S(6)} %select_n.115), kind=kLoop, calls=%fused_computation.62 | loop fusion | flops 18874368 | bytes 37748740 | tf_op jit(solution)/shard_map/convert_element_type | solution.py:147
  617.0 138.1 %reduce-scatter.2.cloned.1.call-done = bf16[256,1536]{0,1:T(8,128)(2,1)} async-done(((bf16[4096,1536]{0,1:T(8,128)(2,1)}), bf16[256,1536]{0,1:T(8,128)(2,1)}) %reduce-scatter.2.cloned.1.call-update) | async-done | bytes 786448 | tf_op jit(solution)/shard_map/reduce_scatter | solution.py:146
  755.1 1.2 convert_element_type.66
  756.5 1.4 copy.35
  (304 shorter events, 62.6 us)
Async XLA Ops:
  7.2 43.9 %all-gather.7.cloned.1.call-start = ((), (), s32[]{:S(2)}) async-start(), calls=%async_computation.3 | async-start | bytes 3342336 | tf_op jit(solution)/shard_map/all_gather | solution.py:86
  7.9 104.9 %all-gather.5.cloned.1.call-start = ((), (), s32[]{:S(2)}) async-start(), calls=%async_computation.2 | async-start | bytes 10027008 | tf_op jit(solution)/shard_map/all_gather | solution.py:85
  8.6 746.4 %reduce-scatter.2.cloned.1.call-start = ((), (), s32[]{:S(2)}) async-start(), calls=%async_computation.1 | async-start | bytes 13369344 | tf_op jit(solution)/shard_map/reduce_scatter | solution.py:146
  114.9 10.4 %collective-permute-start = (bf16[32,4096]{1,0:T(8,128)(2,1)S(1)}, bf16[32,4096]{1,0:T(8,128)(2,1)S(1)}, u32[]{:S(2)}, u32[]{:S(2)}) collective-permute-start(bf16[32,4096]{1,0:T(8,128)(2,1)S(1)} %get-tuple-element.528), channel_id=1, source_target_pairs={{16,0},{32,16},{48,32},{64,48},{80,64},{96,80},{112,96},{128,112},... | collective-permute-start | bytes 786440 | tf_op jit(solution)/shard_map/while/body/eval_jaxpr/ppermute | solution.py:10
  127.0 9.5 %collective-permute-start = (bf16[32,4096]{1,0:T(8,128)(2,1)S(1)}, bf16[32,4096]{1,0:T(8,128)(2,1)S(1)}, u32[]{:S(2)}, u32[]{:S(2)}) collective-permute-start(bf16[32,4096]{1,0:T(8,128)(2,1)S(1)} %get-tuple-element.528), channel_id=1, source_target_pairs={{16,0},{32,16},{48,32},{64,48},{80,64},{96,80},{112,96},{128,112},... | collective-permute-start | bytes 786440 | tf_op jit(solution)/shard_map/while/body/eval_jaxpr/ppermute | solution.py:10
  138.4 16.8 %collective-permute-start = (bf16[32,4096]{1,0:T(8,128)(2,1)S(1)}, bf16[32,4096]{1,0:T(8,128)(2,1)S(1)}, u32[]{:S(2)}, u32[]{:S(2)}) collective-permute-start(bf16[32,4096]{1,0:T(8,128)(2,1)S(1)} %get-tuple-element.528), channel_id=1, source_target_pairs={{16,0},{32,16},{48,32},{64,48},{80,64},{96,80},{112,96},{128,112},... | collective-permute-start | bytes 786440 | tf_op jit(solution)/shard_map/while/body/eval_jaxpr/ppermute | solution.py:10
  156.9 15.9 %collective-permute-start = (bf16[32,4096]{1,0:T(8,128)(2,1)S(1)}, bf16[32,4096]{1,0:T(8,128)(2,1)S(1)}, u32[]{:S(2)}, u32[]{:S(2)}) collective-permute-start(bf16[32,4096]{1,0:T(8,128)(2,1)S(1)} %get-tuple-element.528), channel_id=1, source_target_pairs={{16,0},{32,16},{48,32},{64,48},{80,64},{96,80},{112,96},{128,112},... | collective-permute-start | bytes 786440 | tf_op jit(solution)/shard_map/while/body/eval_jaxpr/ppermute | solution.py:10
  174.7 11.3 %collective-permute-start = (bf16[32,4096]{1,0:T(8,128)(2,1)S(1)}, bf16[32,4096]{1,0:T(8,128)(2,1)S(1)}, u32[]{:S(2)}, u32[]{:S(2)}) collective-permute-start(bf16[32,4096]{1,0:T(8,128)(2,1)S(1)} %get-tuple-element.528), channel_id=1, source_target_pairs={{16,0},{32,16},{48,32},{64,48},{80,64},{96,80},{112,96},{128,112},... | collective-permute-start | bytes 786440 | tf_op jit(solution)/shard_map/while/body/eval_jaxpr/ppermute | solution.py:10
  187.8 10.7 %collective-permute-start = (bf16[32,4096]{1,0:T(8,128)(2,1)S(1)}, bf16[32,4096]{1,0:T(8,128)(2,1)S(1)}, u32[]{:S(2)}, u32[]{:S(2)}) collective-permute-start(bf16[32,4096]{1,0:T(8,128)(2,1)S(1)} %get-tuple-element.528), channel_id=1, source_target_pairs={{16,0},{32,16},{48,32},{64,48},{80,64},{96,80},{112,96},{128,112},... | collective-permute-start | bytes 786440 | tf_op jit(solution)/shard_map/while/body/eval_jaxpr/ppermute | solution.py:10
  200.3 11.0 %collective-permute-start = (bf16[32,4096]{1,0:T(8,128)(2,1)S(1)}, bf16[32,4096]{1,0:T(8,128)(2,1)S(1)}, u32[]{:S(2)}, u32[]{:S(2)}) collective-permute-start(bf16[32,4096]{1,0:T(8,128)(2,1)S(1)} %get-tuple-element.528), channel_id=1, source_target_pairs={{16,0},{32,16},{48,32},{64,48},{80,64},{96,80},{112,96},{128,112},... | collective-permute-start | bytes 786440 | tf_op jit(solution)/shard_map/while/body/eval_jaxpr/ppermute | solution.py:10
  213.1 11.3 %collective-permute-start = (bf16[32,4096]{1,0:T(8,128)(2,1)S(1)}, bf16[32,4096]{1,0:T(8,128)(2,1)S(1)}, u32[]{:S(2)}, u32[]{:S(2)}) collective-permute-start(bf16[32,4096]{1,0:T(8,128)(2,1)S(1)} %get-tuple-element.528), channel_id=1, source_target_pairs={{16,0},{32,16},{48,32},{64,48},{80,64},{96,80},{112,96},{128,112},... | collective-permute-start | bytes 786440 | tf_op jit(solution)/shard_map/while/body/eval_jaxpr/ppermute | solution.py:10
  226.2 14.8 %collective-permute-start = (bf16[32,4096]{1,0:T(8,128)(2,1)S(1)}, bf16[32,4096]{1,0:T(8,128)(2,1)S(1)}, u32[]{:S(2)}, u32[]{:S(2)}) collective-permute-start(bf16[32,4096]{1,0:T(8,128)(2,1)S(1)} %get-tuple-element.528), channel_id=1, source_target_pairs={{16,0},{32,16},{48,32},{64,48},{80,64},{96,80},{112,96},{128,112},... | collective-permute-start | bytes 786440 | tf_op jit(solution)/shard_map/while/body/eval_jaxpr/ppermute | solution.py:10
  242.8 15.3 %collective-permute-start = (bf16[32,4096]{1,0:T(8,128)(2,1)S(1)}, bf16[32,4096]{1,0:T(8,128)(2,1)S(1)}, u32[]{:S(2)}, u32[]{:S(2)}) collective-permute-start(bf16[32,4096]{1,0:T(8,128)(2,1)S(1)} %get-tuple-element.528), channel_id=1, source_target_pairs={{16,0},{32,16},{48,32},{64,48},{80,64},{96,80},{112,96},{128,112},... | collective-permute-start | bytes 786440 | tf_op jit(solution)/shard_map/while/body/eval_jaxpr/ppermute | solution.py:10
  259.9 17.2 %collective-permute-start = (bf16[32,4096]{1,0:T(8,128)(2,1)S(1)}, bf16[32,4096]{1,0:T(8,128)(2,1)S(1)}, u32[]{:S(2)}, u32[]{:S(2)}) collective-permute-start(bf16[32,4096]{1,0:T(8,128)(2,1)S(1)} %get-tuple-element.528), channel_id=1, source_target_pairs={{16,0},{32,16},{48,32},{64,48},{80,64},{96,80},{112,96},{128,112},... | collective-permute-start | bytes 786440 | tf_op jit(solution)/shard_map/while/body/eval_jaxpr/ppermute | solution.py:10
  278.8 13.2 %collective-permute-start = (bf16[32,4096]{1,0:T(8,128)(2,1)S(1)}, bf16[32,4096]{1,0:T(8,128)(2,1)S(1)}, u32[]{:S(2)}, u32[]{:S(2)}) collective-permute-start(bf16[32,4096]{1,0:T(8,128)(2,1)S(1)} %get-tuple-element.528), channel_id=1, source_target_pairs={{16,0},{32,16},{48,32},{64,48},{80,64},{96,80},{112,96},{128,112},... | collective-permute-start | bytes 786440 | tf_op jit(solution)/shard_map/while/body/eval_jaxpr/ppermute | solution.py:10
  293.8 11.0 %collective-permute-start = (bf16[32,4096]{1,0:T(8,128)(2,1)S(1)}, bf16[32,4096]{1,0:T(8,128)(2,1)S(1)}, u32[]{:S(2)}, u32[]{:S(2)}) collective-permute-start(bf16[32,4096]{1,0:T(8,128)(2,1)S(1)} %get-tuple-element.528), channel_id=1, source_target_pairs={{16,0},{32,16},{48,32},{64,48},{80,64},{96,80},{112,96},{128,112},... | collective-permute-start | bytes 786440 | tf_op jit(solution)/shard_map/while/body/eval_jaxpr/ppermute | solution.py:10
  306.7 152.0 %collective-permute-start = (bf16[32,4096]{1,0:T(8,128)(2,1)S(1)}, bf16[32,4096]{1,0:T(8,128)(2,1)S(1)}, u32[]{:S(2)}, u32[]{:S(2)}) collective-permute-start(bf16[32,4096]{1,0:T(8,128)(2,1)S(1)} %get-tuple-element.528), channel_id=1, source_target_pairs={{16,0},{32,16},{48,32},{64,48},{80,64},{96,80},{112,96},{128,112},... | collective-permute-start | bytes 786440 | tf_op jit(solution)/shard_map/while/body/eval_jaxpr/ppermute | solution.py:10
  459.7 10.9 %slice-start = ((s8[9437184]{0:T(1024)(128)(4,1)}), s8[4194304]{0:T(1024)(128)(4,1)S(1)}, s32[]{:S(2)}) async-start(s8[9437184]{0:T(1024)(128)(4,1)} %bitcast.131), calls=%async_computation.4 | async-start | bytes 8388608 | tf_op jit(solution)/shard_map/while/body/eval_jaxpr/cond
  462.3 8.3 %slice-start.1 = ((s8[9437184]{0:T(1024)(128)(4,1)}), s8[4194304]{0:T(1024)(128)(4,1)S(1)}, s32[]{:S(2)}) async-start(s8[9437184]{0:T(1024)(128)(4,1)} %bitcast.131), calls=%async_computation.5 | async-start | bytes 8388608 | tf_op jit(solution)/shard_map/while/body/eval_jaxpr/cond
  462.4 8.3 %slice-start.2 = ((s8[9437184]{0:T(1024)(128)(4,1)}), s8[1048576]{0:T(1024)(128)(4,1)S(1)}, s32[]{:S(2)}) async-start(s8[9437184]{0:T(1024)(128)(4,1)} %bitcast.131), calls=%async_computation.6 | async-start | bytes 2097152 | tf_op jit(solution)/shard_map/while/body/eval_jaxpr/cond
  474.5 12.5 %collective-permute-start = (bf16[32,4096]{1,0:T(8,128)(2,1)S(1)}, bf16[32,4096]{1,0:T(8,128)(2,1)S(1)}, u32[]{:S(2)}, u32[]{:S(2)}) collective-permute-start(bf16[32,4096]{1,0:T(8,128)(2,1)S(1)} %get-tuple-element.528), channel_id=1, source_target_pairs={{16,0},{32,16},{48,32},{64,48},{80,64},{96,80},{112,96},{128,112},... | collective-permute-start | bytes 786440 | tf_op jit(solution)/shard_map/while/body/eval_jaxpr/ppermute | solution.py:10
  488.1 10.9 %slice-start = ((s8[9437184]{0:T(1024)(128)(4,1)}), s8[4194304]{0:T(1024)(128)(4,1)S(1)}, s32[]{:S(2)}) async-start(s8[9437184]{0:T(1024)(128)(4,1)} %bitcast.131), calls=%async_computation.4 | async-start | bytes 8388608 | tf_op jit(solution)/shard_map/while/body/eval_jaxpr/cond
  490.7 8.3 %slice-start.1 = ((s8[9437184]{0:T(1024)(128)(4,1)}), s8[4194304]{0:T(1024)(128)(4,1)S(1)}, s32[]{:S(2)}) async-start(s8[9437184]{0:T(1024)(128)(4,1)} %bitcast.131), calls=%async_computation.5 | async-start | bytes 8388608 | tf_op jit(solution)/shard_map/while/body/eval_jaxpr/cond
  490.7 8.3 %slice-start.2 = ((s8[9437184]{0:T(1024)(128)(4,1)}), s8[1048576]{0:T(1024)(128)(4,1)S(1)}, s32[]{:S(2)}) async-start(s8[9437184]{0:T(1024)(128)(4,1)} %bitcast.131), calls=%async_computation.6 | async-start | bytes 2097152 | tf_op jit(solution)/shard_map/while/body/eval_jaxpr/cond
  502.8 20.3 %collective-permute-start = (bf16[32,4096]{1,0:T(8,128)(2,1)S(1)}, bf16[32,4096]{1,0:T(8,128)(2,1)S(1)}, u32[]{:S(2)}, u32[]{:S(2)}) collective-permute-start(bf16[32,4096]{1,0:T(8,128)(2,1)S(1)} %get-tuple-element.528), channel_id=1, source_target_pairs={{16,0},{32,16},{48,32},{64,48},{80,64},{96,80},{112,96},{128,112},... | collective-permute-start | bytes 786440 | tf_op jit(solution)/shard_map/while/body/eval_jaxpr/ppermute | solution.py:10
  524.2 10.9 %slice-start = ((s8[9437184]{0:T(1024)(128)(4,1)}), s8[4194304]{0:T(1024)(128)(4,1)S(1)}, s32[]{:S(2)}) async-start(s8[9437184]{0:T(1024)(128)(4,1)} %bitcast.131), calls=%async_computation.4 | async-start | bytes 8388608 | tf_op jit(solution)/shard_map/while/body/eval_jaxpr/cond
  526.8 8.3 %slice-start.1 = ((s8[9437184]{0:T(1024)(128)(4,1)}), s8[4194304]{0:T(1024)(128)(4,1)S(1)}, s32[]{:S(2)}) async-start(s8[9437184]{0:T(1024)(128)(4,1)} %bitcast.131), calls=%async_computation.5 | async-start | bytes 8388608 | tf_op jit(solution)/shard_map/while/body/eval_jaxpr/cond
  526.8 8.3 %slice-start.2 = ((s8[9437184]{0:T(1024)(128)(4,1)}), s8[1048576]{0:T(1024)(128)(4,1)S(1)}, s32[]{:S(2)}) async-start(s8[9437184]{0:T(1024)(128)(4,1)} %bitcast.131), calls=%async_computation.6 | async-start | bytes 2097152 | tf_op jit(solution)/shard_map/while/body/eval_jaxpr/cond
  538.9 18.3 %collective-permute-start = (bf16[32,4096]{1,0:T(8,128)(2,1)S(1)}, bf16[32,4096]{1,0:T(8,128)(2,1)S(1)}, u32[]{:S(2)}, u32[]{:S(2)}) collective-permute-start(bf16[32,4096]{1,0:T(8,128)(2,1)S(1)} %get-tuple-element.528), channel_id=1, source_target_pairs={{16,0},{32,16},{48,32},{64,48},{80,64},{96,80},{112,96},{128,112},... | collective-permute-start | bytes 786440 | tf_op jit(solution)/shard_map/while/body/eval_jaxpr/ppermute | solution.py:10
  558.4 10.9 %slice-start = ((s8[9437184]{0:T(1024)(128)(4,1)}), s8[4194304]{0:T(1024)(128)(4,1)S(1)}, s32[]{:S(2)}) async-start(s8[9437184]{0:T(1024)(128)(4,1)} %bitcast.131), calls=%async_computation.4 | async-start | bytes 8388608 | tf_op jit(solution)/shard_map/while/body/eval_jaxpr/cond
  561.0 8.3 %slice-start.1 = ((s8[9437184]{0:T(1024)(128)(4,1)}), s8[4194304]{0:T(1024)(128)(4,1)S(1)}, s32[]{:S(2)}) async-start(s8[9437184]{0:T(1024)(128)(4,1)} %bitcast.131), calls=%async_computation.5 | async-start | bytes 8388608 | tf_op jit(solution)/shard_map/while/body/eval_jaxpr/cond
  561.0 8.3 %slice-start.2 = ((s8[9437184]{0:T(1024)(128)(4,1)}), s8[1048576]{0:T(1024)(128)(4,1)S(1)}, s32[]{:S(2)}) async-start(s8[9437184]{0:T(1024)(128)(4,1)} %bitcast.131), calls=%async_computation.6 | async-start | bytes 2097152 | tf_op jit(solution)/shard_map/while/body/eval_jaxpr/cond
  573.1 8.3 %collective-permute-start = (bf16[32,4096]{1,0:T(8,128)(2,1)S(1)}, bf16[32,4096]{1,0:T(8,128)(2,1)S(1)}, u32[]{:S(2)}, u32[]{:S(2)}) collective-permute-start(bf16[32,4096]{1,0:T(8,128)(2,1)S(1)} %get-tuple-element.528), channel_id=1, source_target_pairs={{16,0},{32,16},{48,32},{64,48},{80,64},{96,80},{112,96},{128,112},... | collective-permute-start | bytes 786440 | tf_op jit(solution)/shard_map/while/body/eval_jaxpr/ppermute | solution.py:10
  583.2 19.8 %collective-permute-start = (bf16[32,4096]{1,0:T(8,128)(2,1)S(1)}, bf16[32,4096]{1,0:T(8,128)(2,1)S(1)}, u32[]{:S(2)}, u32[]{:S(2)}) collective-permute-start(bf16[32,4096]{1,0:T(8,128)(2,1)S(1)} %get-tuple-element.528), channel_id=1, source_target_pairs={{16,0},{32,16},{48,32},{64,48},{80,64},{96,80},{112,96},{128,112},... | collective-permute-start | bytes 786440 | tf_op jit(solution)/shard_map/while/body/eval_jaxpr/ppermute | solution.py:10
  603.0 4.9 copy-start
Sparse Core Ops, SparseCore 0:
  9.8 41.1 all-gather.6
  52.9 59.8 all-gather.4
  617.1 137.9 reduce-scatter.1
where the time goes:
time: 767 us; the launch traced here: 765 us
  waiting for transfers between devices  581 us (76%)
  matrix products  55.9 us (7%)
  starting transfers between devices  52.2 us (7%)
  other arithmetic  37.4 us (5%)
  local copies, waits for them, and re-layouts  22.7 us (3%)
  between operations  14.5 us (2%)
    ppermute x19, waiting for transfers between devices, shifted(): lax.ppermute(value, axis, [(source, source + steps) for source in range(i...  340 us
    reduce_scatter x1, waiting for transfers between devices, shards(): lax.psum_scatter((jnp.concatenate([left_part, right_part], axis=1) * live...  138 us
    all_gather x1, waiting for transfers between devices, shards(): lax.all_gather(w_in[0], 'dp', axis=0, tiled=True)  61.7 us
    ppermute x19, starting transfers between devices, shifted(): lax.ppermute(value, axis, [(source, source + steps) for source in range(i...  52.1 us
    all_gather x1, waiting for transfers between devices, shards(): lax.all_gather(w_out[0], 'dp', axis=0, tiled=True)  39.7 us
    dynamic_update_slice x76, other arithmetic, store(): lax.dynamic_update_index_in_dim(buffer, jnp.where(active, value, older),...  26.2 us
    dot_general x4, matrix products, retention_back(): jnp.dot(inputs, weight_in, preferred_element_type=jnp.float32)  22 us
  transfers between devices with their start and end apart: 22, of which 22 were waited for; matrix products, arithmetic and copies ran while one was open for 1% of the time, Pallas kernels for 0%

commit v1 on v0

--- a/solution.py
+++ b/solution.py
@@ -81,8 +81,12 @@
     replicas = lax.axis_size("dp")
     place = lax.axis_index("section")
     replica = lax.axis_index("dp")
+    _pack_patches = lambda vals, mesh_name: jnp.concatenate(
+        lax.all_to_all(jnp.stack([vals for _ in range(lax.axis_size(mesh_name))]), mesh_name, 0, 0),
+        axis=0,
+    )
     full_in, full_out = (
-        lax.all_gather(w_in[0], "dp", axis=0, tiled=True),
+        _pack_patches(w_in[0], mesh_name="dp"),
         lax.all_gather(w_out[0], "dp", axis=0, tiled=True),
     )
     micro = acts.shape[1]

time: 767 us -> 847 us (1.10)
  local copies, waits for them, and re-layouts: 22.7 us -> 46.9 us
  waiting for transfers between devices: 581 us -> 601 us
  starting transfers between devices: 52.2 us -> 65.5 us
  other arithmetic: 37.4 us -> 49.9 us
  matrix products: 55.9 us -> 64.5 us
    all_gather x1, waiting for transfers between devices: 39.7 us -> 124 us  [shards(): lax.all_gather(w_out[0], 'dp', axis=0, tiled=True)]
    all_gather x1 -> x0, waiting for transfers between devices: 61.7 us -> none  [shards(): lax.all_gather(w_in[0], 'dp', axis=0, tiled=True)]
    dynamic_slice x76, local copies, waits for them, and re-layouts: 1.36 us -> 19.3 us  [store(): older = lax.dynamic_index_in_dim(buffer, which, 0, keepdims=False)]
    dynamic_update_slice x76, other arithmetic: 26.2 us -> 39.4 us  [store(): lax.dynamic_update_index_in_dim(buffer, jnp.where(active, value, older),...]
    dot_general x4, matrix products: 15 us -> 26.4 us  [contract_cols(): lax.dot_general(left, right, (((1,), (1,)), ((), ())), preferred_element_...]
    another operation x48 -> x49, local copies, waits for them, and re-layouts: 10.2 us -> 17.2 us
  transfers between devices with their start and end apart: 22 -> 22, of which waited for: 22 -> 22; matrix products, arithmetic and copies ran while one was open for 1% -> 5% of each run, Pallas kernels for 0% -> 0%
where the time goes in v1:
time: 847 us; the launch traced here: 845 us
  waiting for transfers between devices  601 us (71%)
  starting transfers between devices  65.5 us (8%)
  matrix products  64.5 us (8%)
  other arithmetic  49.9 us (6%)
  local copies, waits for them, and re-layouts  46.9 us (6%)
  between operations  14.8 us (2%)
    ppermute x19, waiting for transfers between devices, shifted(): lax.ppermute(value, axis, [(source, source + steps) for source in range(i...  332 us
    reduce_scatter x1, waiting for transfers between devices, shards(): lax.psum_scatter((jnp.concatenate([left_part, right_part], axis=1) * live...  140 us
    all_gather x1, waiting for transfers between devices, shards(): lax.all_gather(w_out[0], 'dp', axis=0, tiled=True)  124 us
    ppermute x19, starting transfers between devices, shifted(): lax.ppermute(value, axis, [(source, source + steps) for source in range(i...  59.5 us
    dynamic_update_slice x76, other arithmetic, store(): lax.dynamic_update_index_in_dim(buffer, jnp.where(active, value, older),...  39.4 us
    dot_general x4, matrix products, contract_cols(): lax.dot_general(left, right, (((1,), (1,)), ((), ())), preferred_element_...  26.4 us
    dot_general x4, matrix products, retention_back(): jnp.dot(inputs, weight_in, preferred_element_type=jnp.float32)  21.1 us
    dynamic_slice x76, local copies, waits for them, and re-layouts, store(): older = lax.dynamic_index_in_dim(buffer, which, 0, keepdims=False)  19.3 us
  transfers between devices with their start and end apart: 22, of which 22 were waited for; matrix products, arithmetic and copies ran while one was open for 5% of the time, Pallas kernels for 0%

profile of v1, /device:TPU:8, one launch (start us, length us, event | category | flops | bytes accessed | tf_op | source)
XLA Modules:
  0.0 844.7 jit_solution(11814875158643103955)
XLA Ops:
  7.2 6.0 stack.3
  13.1 5.9 all-to-all-start
  21.3 123.9 %all-gather.3.cloned.1.call-done = bf16[1,4096,384]{2,1,0:T(8,128)(2,1)} async-done(((bf16[1,256,384]{2,1,0:T(8,128)(2,1)}), bf16[1,4096,384]{2,1,0:T(8,128)(2,1)}) %all-gather.3.cloned.1.call-update) | async-done | bytes 3145744 | tf_op jit(solution)/shard_map/all_gather | solution.py:90
  145.2 4.8 all-to-all-done
  151.2 530.5 %while.24 = (s32[]{:T(128)}, bf16[32,4096]{1,0:T(8,128)(2,1)S(1)}, bf16[4,32,4096]{2,1,0:T(8,128)(2,1)}, bf16[4,32,1152]{2,1,0:T(8,128)(2,1)S(1)}, bf16[4,32,384...) while((s32[]{:T(128)}, bf16[32,4096]{1,0:T(8,128)(2,1)S(1)}, ...), condition=%wide.region_3.4_spmd.clone, body=%wide.region_0.3_spmd.clone.sunk | while | flops 710326272 | bytes 28613540 | solution.py:143
  153.0 4.1 collective-permute-start
  159.0 3.8 collective-permute-done
  164.6 4.1 collective-permute-start
  170.5 2.9 collective-permute-done
  175.2 4.1 collective-permute-start
  181.2 10.4 %collective-permute-done = bf16[32,4096]{1,0:T(8,128)(2,1)S(1)} collective-permute-done((bf16[32,4096]{1,0:T(8,128)(2,1)S(1)}, bf16[32,4096]{1,0:T(8,128)(2,1)S(1)}, u32[]{:S(2)}, u32[]{:S(2)}) %collective-permute-start) | collective-permute-done | bytes 262176 | tf_op jit(solution)/shard_map/while/body/eval_jaxpr/ppermute | solution.py:10
  193.3 1.9 collective-permute-start
  197.1 7.5 collective-permute-done
  206.5 1.9 collective-permute-start
  210.2 12.3 %collective-permute-done = bf16[32,4096]{1,0:T(8,128)(2,1)S(1)} collective-permute-done((bf16[32,4096]{1,0:T(8,128)(2,1)S(1)}, bf16[32,4096]{1,0:T(8,128)(2,1)S(1)}, u32[]{:S(2)}, u32[]{:S(2)}) %collective-permute-start) | collective-permute-done | bytes 262176 | tf_op jit(solution)/shard_map/while/body/eval_jaxpr/ppermute | solution.py:10
  224.3 1.9 collective-permute-start
  228.1 8.5 %collective-permute-done = bf16[32,4096]{1,0:T(8,128)(2,1)S(1)} collective-permute-done((bf16[32,4096]{1,0:T(8,128)(2,1)S(1)}, bf16[32,4096]{1,0:T(8,128)(2,1)S(1)}, u32[]{:S(2)}, u32[]{:S(2)}) %collective-permute-start) | collective-permute-done | bytes 262176 | tf_op jit(solution)/shard_map/while/body/eval_jaxpr/ppermute | solution.py:10
  238.4 1.9 collective-permute-start
  242.2 6.9 collective-permute-done
  250.9 1.9 collective-permute-start
  254.7 13.5 %collective-permute-done = bf16[32,4096]{1,0:T(8,128)(2,1)S(1)} collective-permute-done((bf16[32,4096]{1,0:T(8,128)(2,1)S(1)}, bf16[32,4096]{1,0:T(8,128)(2,1)S(1)}, u32[]{:S(2)}, u32[]{:S(2)}) %collective-permute-start) | collective-permute-done | bytes 262176 | tf_op jit(solution)/shard_map/while/body/eval_jaxpr/ppermute | solution.py:10
  270.0 1.9 collective-permute-start
  273.8 8.6 %collective-permute-done = bf16[32,4096]{1,0:T(8,128)(2,1)S(1)} collective-permute-done((bf16[32,4096]{1,0:T(8,128)(2,1)S(1)}, bf16[32,4096]{1,0:T(8,128)(2,1)S(1)}, u32[]{:S(2)}, u32[]{:S(2)}) %collective-permute-start) | collective-permute-done | bytes 262176 | tf_op jit(solution)/shard_map/while/body/eval_jaxpr/ppermute | solution.py:10
  284.2 1.9 collective-permute-start
  287.9 11.3 %collective-permute-done = bf16[32,4096]{1,0:T(8,128)(2,1)S(1)} collective-permute-done((bf16[32,4096]{1,0:T(8,128)(2,1)S(1)}, bf16[32,4096]{1,0:T(8,128)(2,1)S(1)}, u32[]{:S(2)}, u32[]{:S(2)}) %collective-permute-start) | collective-permute-done | bytes 262176 | tf_op jit(solution)/shard_map/while/body/eval_jaxpr/ppermute | solution.py:10
  301.0 1.9 collective-permute-start
  304.8 8.1 collective-permute-done
  314.6 1.9 collective-permute-start
  318.4 7.5 collective-permute-done
  327.7 1.9 collective-permute-start
  331.5 7.5 collective-permute-done
  340.8 1.9 collective-permute-start
  344.6 185.4 %collective-permute-done = bf16[32,4096]{1,0:T(8,128)(2,1)S(1)} collective-permute-done((bf16[32,4096]{1,0:T(8,128)(2,1)S(1)}, bf16[32,4096]{1,0:T(8,128)(2,1)S(1)}, u32[]{:S(2)}, u32[]{:S(2)}) %collective-permute-start) | collective-permute-done | bytes 262176 | tf_op jit(solution)/shard_map/while/body/eval_jaxpr/ppermute | solution.py:10
  531.0 17.1 %conditional.3 = (bf16[32,4096]{1,0:T(8,128)(2,1)S(1)}, bf16[32,1152]{1,0:T(8,128)(2,1)}, bf16[32,384]{1,0:T(8,128)(2,1)S(1)}) conditional(s32[]{:T(128)} %convert_element_type.90, () %tuple.68, (bf16[32,4096]{1,0:T(8,128)(2,1)S(1)}, bf16[4,32,4096]{2,1,0:T(8,128)(2,1)S(1)}, s32[]{:T(128)}, bf16[4096,1152]{1,0:T(8,128)(2,1)}, ...), branch_computations={%region_1.1_spmd, %region_2.2_spmd.clone} | conditional | flops 709883904 | bytes 23926836 | solution.py:126
  531.0 2.4 fusion.7
  533.5 5.3 convolution_convert_fusion
  541.6 6.6 fusion.2
  548.2 1.9 collective-permute-start
  552.8 8.0 collective-permute-done
  561.9 17.1 %conditional.3 = (bf16[32,4096]{1,0:T(8,128)(2,1)S(1)}, bf16[32,1152]{1,0:T(8,128)(2,1)}, bf16[32,384]{1,0:T(8,128)(2,1)S(1)}) conditional(s32[]{:T(128)} %convert_element_type.90, () %tuple.68, (bf16[32,4096]{1,0:T(8,128)(2,1)S(1)}, bf16[4,32,4096]{2,1,0:T(8,128)(2,1)S(1)}, s32[]{:T(128)}, bf16[4096,1152]{1,0:T(8,128)(2,1)}, ...), branch_computations={%region_1.1_spmd, %region_2.2_spmd.clone} | conditional | flops 709883904 | bytes 23926836 | solution.py:126
  561.9 2.4 fusion.7
  564.4 5.3 convolution_convert_fusion
  572.5 6.6 fusion.2
  579.1 1.9 collective-permute-start
  583.7 12.2 %collective-permute-done = bf16[32,4096]{1,0:T(8,128)(2,1)S(1)} collective-permute-done((bf16[32,4096]{1,0:T(8,128)(2,1)S(1)}, bf16[32,4096]{1,0:T(8,128)(2,1)S(1)}, u32[]{:S(2)}, u32[]{:S(2)}) %collective-permute-start) | collective-permute-done | bytes 262176 | tf_op jit(solution)/shard_map/while/body/eval_jaxpr/ppermute | solution.py:10
  597.0 17.1 %conditional.3 = (bf16[32,4096]{1,0:T(8,128)(2,1)S(1)}, bf16[32,1152]{1,0:T(8,128)(2,1)}, bf16[32,384]{1,0:T(8,128)(2,1)S(1)}) conditional(s32[]{:T(128)} %convert_element_type.90, () %tuple.68, (bf16[32,4096]{1,0:T(8,128)(2,1)S(1)}, bf16[4,32,4096]{2,1,0:T(8,128)(2,1)S(1)}, s32[]{:T(128)}, bf16[4096,1152]{1,0:T(8,128)(2,1)}, ...), branch_computations={%region_1.1_spmd, %region_2.2_spmd.clone} | conditional | flops 709883904 | bytes 23926836 | solution.py:126
  597.0 2.4 fusion.7
  599.5 5.3 convolution_convert_fusion
  607.6 6.6 fusion.2
  614.2 1.9 collective-permute-start
  618.8 12.4 %collective-permute-done = bf16[32,4096]{1,0:T(8,128)(2,1)S(1)} collective-permute-done((bf16[32,4096]{1,0:T(8,128)(2,1)S(1)}, bf16[32,4096]{1,0:T(8,128)(2,1)S(1)}, u32[]{:S(2)}, u32[]{:S(2)}) %collective-permute-start) | collective-permute-done | bytes 262176 | tf_op jit(solution)/shard_map/while/body/eval_jaxpr/ppermute | solution.py:10
  632.3 17.1 %conditional.3 = (bf16[32,4096]{1,0:T(8,128)(2,1)S(1)}, bf16[32,1152]{1,0:T(8,128)(2,1)}, bf16[32,384]{1,0:T(8,128)(2,1)S(1)}) conditional(s32[]{:T(128)} %convert_element_type.90, () %tuple.68, (bf16[32,4096]{1,0:T(8,128)(2,1)S(1)}, bf16[4,32,4096]{2,1,0:T(8,128)(2,1)S(1)}, s32[]{:T(128)}, bf16[4096,1152]{1,0:T(8,128)(2,1)}, ...), branch_computations={%region_1.1_spmd, %region_2.2_spmd.clone} | conditional | flops 709883904 | bytes 23926836 | solution.py:126
  632.3 2.4 fusion.7
  634.8 5.3 convolution_convert_fusion
  642.9 6.6 fusion.2
  649.5 1.9 collective-permute-start
  654.1 3.6 collective-permute-done
  659.5 18.4 %collective-permute-start = (bf16[32,4096]{1,0:T(8,128)(2,1)S(1)}, bf16[32,4096]{1,0:T(8,128)(2,1)S(1)}, u32[]{:S(2)}, u32[]{:S(2)}) collective-permute-start(bf16[32,4096]{1,0:T(8,128)(2,1)S(1)} %get-tuple-element.528), channel_id=1, source_target_pairs={{16,0},{32,16},{48,32},{64,48},{80,64},{96,80},{112,96},{128,112},... | collective-permute-start | bytes 786440 | tf_op jit(solution)/shard_map/while/body/eval_jaxpr/ppermute | solution.py:10
  679.8 2.0 collective-permute-done
  682.8 2.6 convolution_bitcast_fusion
  685.4 9.0 %fusion.32 = bf16[4096,1536]{0,1:T(8,128)(2,1)} fusion(f32[4096,384]{0,1:T(8,128)S(1)} %convolution_bitcast_fusion.1, f32[4096,1152]{0,1:T(8,128)S(1)} %convolution_bitcast_fusion, f32[]{:T(128)S(6)} %select_n.115), kind=kLoop, calls=%fused_computation.62 | loop fusion | flops 18874368 | bytes 37748740 | tf_op jit(solution)/shard_map/convert_element_type | solution.py:151
  694.5 139.7 %reduce-scatter.2.cloned.1.call-done = bf16[256,1536]{0,1:T(8,128)(2,1)} async-done(((bf16[4096,1536]{0,1:T(8,128)(2,1)}), bf16[256,1536]{0,1:T(8,128)(2,1)}) %reduce-scatter.2.cloned.1.call-update) | async-done | bytes 786448 | tf_op jit(solution)/shard_map/reduce_scatter | solution.py:150
  834.2 1.2 convert_element_type.66
  835.6 1.4 copy.35
  (280 shorter events, 95.0 us)
Async XLA Ops:
  13.1 6.7 copy-start.1
  13.1 8.0 copy-start.2
  13.1 138.1 %copy-start = (bf16[1,4,32,4096]{3,2,1,0:T(8,128)(2,1)S(1)}, bf16[1,4,32,4096]{3,2,1,0:T(8,128)(2,1)}, u32[]{:S(2)}) copy-start(bf16[1,4,32,4096]{3,2,1,0:T(8,128)(2,1)} %param.10) | copy-start | bytes 3145732
  13.1 136.8 %all-to-all-start = ((bf16[16,256,1152]{2,1,0:T(8,128)(2,1)}), bf16[16,256,1152]{2,1,0:T(8,128)(2,1)}, u32[]{:S(2)}, u32[]{:S(2)}) async-start(bf16[16,256,1152]{2,1,0:T(8,128)(2,1)} %stack.3), calls=%async_computation | async-start | bytes 18874368 | tf_op jit(solution)/shard_map/all_to_all | solution.py:85
  19.1 126.1 %all-gather.3.cloned.1.call-start = ((), (), s32[]{:S(2)}) async-start(), calls=%async_computation.3 | async-start | bytes 3342336 | tf_op jit(solution)/shard_map/all_gather | solution.py:90
  19.8 814.3 %reduce-scatter.2.cloned.1.call-start = ((), (), s32[]{:S(2)}) async-start(), calls=%async_computation.2 | async-start | bytes 13369344 | tf_op jit(solution)/shard_map/reduce_scatter | solution.py:150
  153.0 9.7 %collective-permute-start = (bf16[32,4096]{1,0:T(8,128)(2,1)S(1)}, bf16[32,4096]{1,0:T(8,128)(2,1)S(1)}, u32[]{:S(2)}, u32[]{:S(2)}) collective-permute-start(bf16[32,4096]{1,0:T(8,128)(2,1)S(1)} %get-tuple-element.528), channel_id=1, source_target_pairs={{16,0},{32,16},{48,32},{64,48},{80,64},{96,80},{112,96},{128,112},... | collective-permute-start | bytes 786440 | tf_op jit(solution)/shard_map/while/body/eval_jaxpr/ppermute | solution.py:10
  164.6 8.8 %collective-permute-start = (bf16[32,4096]{1,0:T(8,128)(2,1)S(1)}, bf16[32,4096]{1,0:T(8,128)(2,1)S(1)}, u32[]{:S(2)}, u32[]{:S(2)}) collective-permute-start(bf16[32,4096]{1,0:T(8,128)(2,1)S(1)} %get-tuple-element.528), channel_id=1, source_target_pairs={{16,0},{32,16},{48,32},{64,48},{80,64},{96,80},{112,96},{128,112},... | collective-permute-start | bytes 786440 | tf_op jit(solution)/shard_map/while/body/eval_jaxpr/ppermute | solution.py:10
  175.2 16.3 %collective-permute-start = (bf16[32,4096]{1,0:T(8,128)(2,1)S(1)}, bf16[32,4096]{1,0:T(8,128)(2,1)S(1)}, u32[]{:S(2)}, u32[]{:S(2)}) collective-permute-start(bf16[32,4096]{1,0:T(8,128)(2,1)S(1)} %get-tuple-element.528), channel_id=1, source_target_pairs={{16,0},{32,16},{48,32},{64,48},{80,64},{96,80},{112,96},{128,112},... | collective-permute-start | bytes 786440 | tf_op jit(solution)/shard_map/while/body/eval_jaxpr/ppermute | solution.py:10
  193.3 11.3 %collective-permute-start = (bf16[32,4096]{1,0:T(8,128)(2,1)S(1)}, bf16[32,4096]{1,0:T(8,128)(2,1)S(1)}, u32[]{:S(2)}, u32[]{:S(2)}) collective-permute-start(bf16[32,4096]{1,0:T(8,128)(2,1)S(1)} %get-tuple-element.528), channel_id=1, source_target_pairs={{16,0},{32,16},{48,32},{64,48},{80,64},{96,80},{112,96},{128,112},... | collective-permute-start | bytes 786440 | tf_op jit(solution)/shard_map/while/body/eval_jaxpr/ppermute | solution.py:10
  206.5 16.1 %collective-permute-start = (bf16[32,4096]{1,0:T(8,128)(2,1)S(1)}, bf16[32,4096]{1,0:T(8,128)(2,1)S(1)}, u32[]{:S(2)}, u32[]{:S(2)}) collective-permute-start(bf16[32,4096]{1,0:T(8,128)(2,1)S(1)} %get-tuple-element.528), channel_id=1, source_target_pairs={{16,0},{32,16},{48,32},{64,48},{80,64},{96,80},{112,96},{128,112},... | collective-permute-start | bytes 786440 | tf_op jit(solution)/shard_map/while/body/eval_jaxpr/ppermute | solution.py:10
  224.3 12.3 %collective-permute-start = (bf16[32,4096]{1,0:T(8,128)(2,1)S(1)}, bf16[32,4096]{1,0:T(8,128)(2,1)S(1)}, u32[]{:S(2)}, u32[]{:S(2)}) collective-permute-start(bf16[32,4096]{1,0:T(8,128)(2,1)S(1)} %get-tuple-element.528), channel_id=1, source_target_pairs={{16,0},{32,16},{48,32},{64,48},{80,64},{96,80},{112,96},{128,112},... | collective-permute-start | bytes 786440 | tf_op jit(solution)/shard_map/while/body/eval_jaxpr/ppermute | solution.py:10
  238.4 10.7 %collective-permute-start = (bf16[32,4096]{1,0:T(8,128)(2,1)S(1)}, bf16[32,4096]{1,0:T(8,128)(2,1)S(1)}, u32[]{:S(2)}, u32[]{:S(2)}) collective-permute-start(bf16[32,4096]{1,0:T(8,128)(2,1)S(1)} %get-tuple-element.528), channel_id=1, source_target_pairs={{16,0},{32,16},{48,32},{64,48},{80,64},{96,80},{112,96},{128,112},... | collective-permute-start | bytes 786440 | tf_op jit(solution)/shard_map/while/body/eval_jaxpr/ppermute | solution.py:10
  250.9 17.3 %collective-permute-start = (bf16[32,4096]{1,0:T(8,128)(2,1)S(1)}, bf16[32,4096]{1,0:T(8,128)(2,1)S(1)}, u32[]{:S(2)}, u32[]{:S(2)}) collective-permute-start(bf16[32,4096]{1,0:T(8,128)(2,1)S(1)} %get-tuple-element.528), channel_id=1, source_target_pairs={{16,0},{32,16},{48,32},{64,48},{80,64},{96,80},{112,96},{128,112},... | collective-permute-start | bytes 786440 | tf_op jit(solution)/shard_map/while/body/eval_jaxpr/ppermute | solution.py:10
  270.0 12.4 %collective-permute-start = (bf16[32,4096]{1,0:T(8,128)(2,1)S(1)}, bf16[32,4096]{1,0:T(8,128)(2,1)S(1)}, u32[]{:S(2)}, u32[]{:S(2)}) collective-permute-start(bf16[32,4096]{1,0:T(8,128)(2,1)S(1)} %get-tuple-element.528), channel_id=1, source_target_pairs={{16,0},{32,16},{48,32},{64,48},{80,64},{96,80},{112,96},{128,112},... | collective-permute-start | bytes 786440 | tf_op jit(solution)/shard_map/while/body/eval_jaxpr/ppermute | solution.py:10
  284.2 15.0 %collective-permute-start = (bf16[32,4096]{1,0:T(8,128)(2,1)S(1)}, bf16[32,4096]{1,0:T(8,128)(2,1)S(1)}, u32[]{:S(2)}, u32[]{:S(2)}) collective-permute-start(bf16[32,4096]{1,0:T(8,128)(2,1)S(1)} %get-tuple-element.528), channel_id=1, source_target_pairs={{16,0},{32,16},{48,32},{64,48},{80,64},{96,80},{112,96},{128,112},... | collective-permute-start | bytes 786440 | tf_op jit(solution)/shard_map/while/body/eval_jaxpr/ppermute | solution.py:10
  301.0 11.9 %collective-permute-start = (bf16[32,4096]{1,0:T(8,128)(2,1)S(1)}, bf16[32,4096]{1,0:T(8,128)(2,1)S(1)}, u32[]{:S(2)}, u32[]{:S(2)}) collective-permute-start(bf16[32,4096]{1,0:T(8,128)(2,1)S(1)} %get-tuple-element.528), channel_id=1, source_target_pairs={{16,0},{32,16},{48,32},{64,48},{80,64},{96,80},{112,96},{128,112},... | collective-permute-start | bytes 786440 | tf_op jit(solution)/shard_map/while/body/eval_jaxpr/ppermute | solution.py:10
  314.6 11.3 %collective-permute-start = (bf16[32,4096]{1,0:T(8,128)(2,1)S(1)}, bf16[32,4096]{1,0:T(8,128)(2,1)S(1)}, u32[]{:S(2)}, u32[]{:S(2)}) collective-permute-start(bf16[32,4096]{1,0:T(8,128)(2,1)S(1)} %get-tuple-element.528), channel_id=1, source_target_pairs={{16,0},{32,16},{48,32},{64,48},{80,64},{96,80},{112,96},{128,112},... | collective-permute-start | bytes 786440 | tf_op jit(solution)/shard_map/while/body/eval_jaxpr/ppermute | solution.py:10
  327.7 11.3 %collective-permute-start = (bf16[32,4096]{1,0:T(8,128)(2,1)S(1)}, bf16[32,4096]{1,0:T(8,128)(2,1)S(1)}, u32[]{:S(2)}, u32[]{:S(2)}) collective-permute-start(bf16[32,4096]{1,0:T(8,128)(2,1)S(1)} %get-tuple-element.528), channel_id=1, source_target_pairs={{16,0},{32,16},{48,32},{64,48},{80,64},{96,80},{112,96},{128,112},... | collective-permute-start | bytes 786440 | tf_op jit(solution)/shard_map/while/body/eval_jaxpr/ppermute | solution.py:10
  340.8 189.2 %collective-permute-start = (bf16[32,4096]{1,0:T(8,128)(2,1)S(1)}, bf16[32,4096]{1,0:T(8,128)(2,1)S(1)}, u32[]{:S(2)}, u32[]{:S(2)}) collective-permute-start(bf16[32,4096]{1,0:T(8,128)(2,1)S(1)} %get-tuple-element.528), channel_id=1, source_target_pairs={{16,0},{32,16},{48,32},{64,48},{80,64},{96,80},{112,96},{128,112},... | collective-permute-start | bytes 786440 | tf_op jit(solution)/shard_map/while/body/eval_jaxpr/ppermute | solution.py:10
  548.2 12.7 %collective-permute-start = (bf16[32,4096]{1,0:T(8,128)(2,1)S(1)}, bf16[32,4096]{1,0:T(8,128)(2,1)S(1)}, u32[]{:S(2)}, u32[]{:S(2)}) collective-permute-start(bf16[32,4096]{1,0:T(8,128)(2,1)S(1)} %get-tuple-element.528), channel_id=1, source_target_pairs={{16,0},{32,16},{48,32},{64,48},{80,64},{96,80},{112,96},{128,112},... | collective-permute-start | bytes 786440 | tf_op jit(solution)/shard_map/while/body/eval_jaxpr/ppermute | solution.py:10
  579.1 16.9 %collective-permute-start = (bf16[32,4096]{1,0:T(8,128)(2,1)S(1)}, bf16[32,4096]{1,0:T(8,128)(2,1)S(1)}, u32[]{:S(2)}, u32[]{:S(2)}) collective-permute-start(bf16[32,4096]{1,0:T(8,128)(2,1)S(1)} %get-tuple-element.528), channel_id=1, source_target_pairs={{16,0},{32,16},{48,32},{64,48},{80,64},{96,80},{112,96},{128,112},... | collective-permute-start | bytes 786440 | tf_op jit(solution)/shard_map/while/body/eval_jaxpr/ppermute | solution.py:10
  614.2 17.1 %collective-permute-start = (bf16[32,4096]{1,0:T(8,128)(2,1)S(1)}, bf16[32,4096]{1,0:T(8,128)(2,1)S(1)}, u32[]{:S(2)}, u32[]{:S(2)}) collective-permute-start(bf16[32,4096]{1,0:T(8,128)(2,1)S(1)} %get-tuple-element.528), channel_id=1, source_target_pairs={{16,0},{32,16},{48,32},{64,48},{80,64},{96,80},{112,96},{128,112},... | collective-permute-start | bytes 786440 | tf_op jit(solution)/shard_map/while/body/eval_jaxpr/ppermute | solution.py:10
  649.5 8.3 collective-permute-start
  659.5 22.2 %collective-permute-start = (bf16[32,4096]{1,0:T(8,128)(2,1)S(1)}, bf16[32,4096]{1,0:T(8,128)(2,1)S(1)}, u32[]{:S(2)}, u32[]{:S(2)}) collective-permute-start(bf16[32,4096]{1,0:T(8,128)(2,1)S(1)} %get-tuple-element.528), channel_id=1, source_target_pairs={{16,0},{32,16},{48,32},{64,48},{80,64},{96,80},{112,96},{128,112},... | collective-permute-start | bytes 786440 | tf_op jit(solution)/shard_map/while/body/eval_jaxpr/ppermute | solution.py:10
Sparse Core Ops, SparseCore 0:
  21.8 123.3 all-gather.2
  694.6 139.5 reduce-scatter.1
